TPU v7x, 32 devices: a whole 2x2x4 slice. The times are simulated.
32 devices in a mesh: seq: 8 (over z, x), head: 4 (over y, core).
Axes of the slice: x: 2, y: 2, z: 4, core: 2. Of those that a mesh axis runs over, the one named last changes fastest.
Arguments:
- history: bfloat16 [6144, 1024], P('seq'), may hold values from -6 to 6
- ln_gain: bfloat16 [1024], replicated, may hold values from 0.5 to 1.5
- w_in: bfloat16 [4, 1024, 1024], P(None, None, 'head'), may hold values from -0.1875 to 0.1875
- out_gain: bfloat16 [1024], P('head'), may hold values from 0.5 to 1.5
- w_out: bfloat16 [1024, 1024], P('head'), may hold values from -0.25 to 0.25
- block_lists: int32 [48, 16], P('seq'), may hold values from 0 to 47, as said below
- counts: int32 [48], P('seq'), may hold values from 1 to 16, as said below
Outputs:
- mixed: bfloat16 [6144, 1024], P('seq', 'head')
Inputs may be any that keep to these rules, and one draw needn't show every extreme that they name: For query block b, entries 0 to counts[b] - 1 of block_lists[b] are distinct blocks from max(0, b - 31) to b, and entry 0 is b itself; later entries equal b and are not live. counts[b] is at most min(16, b + 1); the last block has min(16, 32, 48) live entries.
All inputs are finite; a program needn't handle non-finite values.
Results may differ from a plain program's by a relative error of at most 0.008.
Values may be sent and summed in bfloat16 or wider, within the bound.
No kernel may reach another device: no remote copies, remote signals or barrier semaphores. Data moves between devices by JAX's collectives and lax.ppermute only.
A program may use at most 64 MiB of HBM per device.

v0:
```python
import jax
import jax.numpy as jnp
from jax import lax
from jax.sharding import PartitionSpec as P

DH = 128
WIN = 32
MAXK = 16


EPS = 1e-05


def shifted(shard, axis, by):
    length = lax.axis_size(axis)
    pairs = [(i, i + by) for i in range(length) if 0 <= i + by < length]
    return lax.ppermute(shard, axis, pairs)


def body(history, ln_gain, w_in, out_gain, w_out, block_lists, counts):
    tok_rows, width = history.shape
    blocks_dev = counts.shape[0]
    block_rows = tok_rows // blocks_dev
    head_cols = w_in.shape[2]
    heads_dev = head_cols // DH
    scale = DH ** (-0.5)
    floats = history.astype(jnp.float32)
    centre = jnp.mean(floats, axis=-1, keepdims=True)
    spread_sq = jnp.mean(jnp.square(floats - centre), axis=-1, keepdims=True)
    normed_x = (
        (floats - centre) * lax.rsqrt(spread_sq + EPS) * ln_gain.astype(jnp.float32)
    ).astype(jnp.bfloat16)
    projected = jnp.einsum("td,pde->pte", normed_x, w_in, preferred_element_type=jnp.float32)
    projected = jax.nn.silu(projected).astype(jnp.bfloat16)
    gating = projected[0]
    queries = projected[2]
    keys_values = jnp.stack([projected[3], projected[1]])
    seq_index = lax.axis_index("seq")
    reach_devs = (WIN - 1 + blocks_dev - 1) // blocks_dev
    depth = reach_devs + 1

    def advance(carried, unused):
        arrived = shifted(carried, "seq", 1)
        return (arrived, arrived)

    last_one, earlier = lax.scan(advance, keys_values, None, length=reach_devs)
    window = jnp.concatenate([keys_values[None], earlier], axis=0)
    in_list = jnp.arange(MAXK, dtype=jnp.int32)[None, :] < counts[:, None]
    queries_h = queries.reshape(tok_rows, heads_dev, DH)
    rows_here = jnp.arange(tok_rows, dtype=jnp.int32)

    def visit(attended, item):
        visiting, offset = item
        source = seq_index - offset
        key_ids = source * blocks_dev + jnp.arange(blocks_dev, dtype=jnp.int32)
        member = jnp.any(
            in_list[:, :, None] & (block_lists[:, :, None] == key_ids[None, None, :]), axis=1
        )
        member_rows = jnp.broadcast_to(
            member[:, None, :, None], (blocks_dev, block_rows, blocks_dev, block_rows)
        )
        member_rows = member_rows.reshape(tok_rows, tok_rows)
        causal = (source * tok_rows + rows_here)[None, :] <= (seq_index * tok_rows + rows_here)[
            :, None
        ]
        allowed = member_rows & causal
        visit_keys = visiting[0].reshape(tok_rows, heads_dev, DH)
        visit_values = visiting[1].reshape(tok_rows, heads_dev, DH)
        scores = (
            jnp.einsum("qhe,khe->hqk", queries_h, visit_keys, preferred_element_type=jnp.float32)
            * scale
        )
        weights = jnp.where(allowed[None], jax.nn.silu(scores), 0.0).astype(jnp.bfloat16)
        update = jnp.einsum(
            "hqk,khe->qhe", weights, visit_values, preferred_element_type=jnp.float32
        )
        return (attended + update, None)

    start = jnp.zeros((tok_rows, heads_dev, DH), jnp.float32)
    attended, unused = lax.scan(visit, start, (window, jnp.arange(depth, dtype=jnp.int32)))
    centre_h = jnp.mean(attended, axis=-1, keepdims=True)
    spread_h = jnp.mean(jnp.square(attended - centre_h), axis=-1, keepdims=True)
    normed_h = (attended - centre_h) * lax.rsqrt(spread_h + EPS)
    gated = (
        normed_h
        * out_gain.astype(jnp.float32).reshape(heads_dev, DH)
        * gating.astype(jnp.float32).reshape(tok_rows, heads_dev, DH)
    )
    gated = gated.astype(jnp.bfloat16).reshape(tok_rows, head_cols)
    partial_terms = jnp.dot(gated, w_out, preferred_element_type=jnp.float32)
    summed = lax.psum_scatter(partial_terms, "head", scatter_dimension=1, tiled=True)
    columns = width // lax.axis_size("head")
    residual = lax.dynamic_slice_in_dim(history, lax.axis_index("head") * columns, columns, 1)
    return (summed + residual.astype(jnp.float32)).astype(jnp.bfloat16)


def solution(mesh):
    placed = (
        P("seq", None),
        P(),
        P(None, None, "head"),
        P("head"),
        P("head", None),
        P("seq", None),
        P("seq"),
    )
    return jax.shard_map(
        body, mesh=mesh, in_specs=placed, out_specs=P("seq", "head"), check_vma=False
    )
```

profile of v0, /device:TPU:25, one launch (start us, length us, event | category | flops | bytes accessed | tf_op | source)
XLA Modules:
  0.0 283.8 jit_solution(8406084769966407841)
XLA Ops:
  6.6 1.8 convert_reduce_fusion
  8.4 2.0 fusion.24
  10.4 2.5 fusion.30
  16.8 139.4 %while.25 = (s32[]{:T(128)}, bf16[2,768,256]{2,1,0:T(8,128)(2,1)}, bf16[6,2,768,256]{2,3,1,0:T(8,128)(2,1)}, s32[]{:T(128)}) while((s32[]{:T(128)}, bf16[2,768,256]{2,1,0:T(8,128)(2,1)}, bf16[6,2,768,256]{2,3,1,0:T(8,128)(2,1)}, s32[]{:T(128)}) %tuple.58), condition=%wide.region_3.4_spmd, body=%wide.region_2.3_spmd.sunk | while | flops 2 | bytes 7864425 | solution.py:46
  16.8 3.1 %collective-permute-start = (bf16[2,768,256]{2,1,0:T(8,128)(2,1)}, bf16[2,768,256]{2,1,0:T(8,128)(2,1)S(1)}, u32[]{:S(2)}, u32[]{:S(2)}) collective-permute-start(bf16[2,768,256]{2,1,0:T(8,128)(2,1)} %get-tuple-element.331), channel_id=1, source_target_pairs={{0,4},{4,8},{8,12},{12,16},{16,20},{20,24},{24,28},{1,5},{5,9},{9,... | collective-permute-start | bytes 2359304 | tf_op jit(solution)/shard_map/while/body/eval_jaxpr/ppermute | solution.py:17
  19.9 18.3 %collective-permute-done = bf16[2,768,256]{2,1,0:T(8,128)(2,1)S(1)} collective-permute-done((bf16[2,768,256]{2,1,0:T(8,128)(2,1)}, bf16[2,768,256]{2,1,0:T(8,128)(2,1)S(1)}, u32[]{:S(2)}, u32[]{:S(2)}) %collective-permute-start) | collective-permute-done | bytes 786464 | tf_op jit(solution)/shard_map/while/body/eval_jaxpr/ppermute | solution.py:17
  38.2 1.2 copy.37
  39.4 2.1 constant_dynamic-update-slice_fusion.2
  42.4 2.2 collective-permute-start
  44.6 18.3 %collective-permute-done = bf16[2,768,256]{2,1,0:T(8,128)(2,1)S(1)} collective-permute-done((bf16[2,768,256]{2,1,0:T(8,128)(2,1)}, bf16[2,768,256]{2,1,0:T(8,128)(2,1)S(1)}, u32[]{:S(2)}, u32[]{:S(2)}) %collective-permute-start) | collective-permute-done | bytes 786464 | tf_op jit(solution)/shard_map/while/body/eval_jaxpr/ppermute | solution.py:17
  62.9 1.2 copy.37
  64.0 2.1 constant_dynamic-update-slice_fusion.2
  67.0 1.9 collective-permute-start
  68.9 17.6 %collective-permute-done = bf16[2,768,256]{2,1,0:T(8,128)(2,1)S(1)} collective-permute-done((bf16[2,768,256]{2,1,0:T(8,128)(2,1)}, bf16[2,768,256]{2,1,0:T(8,128)(2,1)S(1)}, u32[]{:S(2)}, u32[]{:S(2)}) %collective-permute-start) | collective-permute-done | bytes 786464 | tf_op jit(solution)/shard_map/while/body/eval_jaxpr/ppermute | solution.py:17
  87.7 2.1 constant_dynamic-update-slice_fusion.2
  90.6 1.9 collective-permute-start
  92.5 16.7 %collective-permute-done = bf16[2,768,256]{2,1,0:T(8,128)(2,1)S(1)} collective-permute-done((bf16[2,768,256]{2,1,0:T(8,128)(2,1)}, bf16[2,768,256]{2,1,0:T(8,128)(2,1)S(1)}, u32[]{:S(2)}, u32[]{:S(2)}) %collective-permute-start) | collective-permute-done | bytes 786464 | tf_op jit(solution)/shard_map/while/body/eval_jaxpr/ppermute | solution.py:17
  110.4 2.1 constant_dynamic-update-slice_fusion.2
  113.4 1.9 collective-permute-start
  115.3 15.8 %collective-permute-done = bf16[2,768,256]{2,1,0:T(8,128)(2,1)S(1)} collective-permute-done((bf16[2,768,256]{2,1,0:T(8,128)(2,1)}, bf16[2,768,256]{2,1,0:T(8,128)(2,1)S(1)}, u32[]{:S(2)}, u32[]{:S(2)}) %collective-permute-start) | collective-permute-done | bytes 786464 | tf_op jit(solution)/shard_map/while/body/eval_jaxpr/ppermute | solution.py:17
  131.1 1.2 copy.37
  132.3 2.2 constant_dynamic-update-slice_fusion.2
  135.3 1.9 collective-permute-start
  137.2 14.9 %collective-permute-done = bf16[2,768,256]{2,1,0:T(8,128)(2,1)S(1)} collective-permute-done((bf16[2,768,256]{2,1,0:T(8,128)(2,1)}, bf16[2,768,256]{2,1,0:T(8,128)(2,1)S(1)}, u32[]{:S(2)}, u32[]{:S(2)}) %collective-permute-start) | collective-permute-done | bytes 786464 | tf_op jit(solution)/shard_map/while/body/eval_jaxpr/ppermute | solution.py:17
  152.1 1.2 copy.37
  153.3 2.1 constant_dynamic-update-slice_fusion.2
  156.2 5.4 %pad_maximum_fusion = bf16[7,2,768,256]{2,3,1,0:T(8,128)(2,1)} fusion(bf16[6,2,768,256]{2,3,1,0:T(8,128)(2,1)} %get-tuple-element.113, bf16[1,2,768,256]{2,3,1,0:T(8,128)(2,1)} %get-tuple-element.242), kind=kLoop, calls=%fused_computation.25 | loop fusion | flops 2752512 | bytes 11010048 | tf_op jit(solution)/shard_map/concatenate | solution.py:47
  161.7 63.3 %while.26 = (s32[]{:T(128)}, f32[768,2,128]{0,2,1:T(8,128)}, bf16[7,2,768,256]{2,3,1,0:T(8,128)(2,1)}, s32[6,16]{1,0:T(8,128)S(1)}, s32[7]{0:T(128)S(1)}, /*inde...) while((s32[]{:T(128)}, f32[768,2,128]{0,2,1:T(8,128)}, ...), condition=%wide.region_6.7_spmd.clone.clone, body=%wide.region_4.6_spmd.clone.clone.sunk | while | flops 613813504 | bytes 7877551 | solution.py:80
  165.1 1.2 constant_dynamic-slice_fusion.3
  166.3 4.2 %fusion.55 = f32[768,2,128]{0,2,1:T(8,128)} fusion(bf16[768,2,128]{0,2,1:T(8,128)(2,1)S(1)} %bitcast.88, pred[768,768]{0,1:T(8,128)(4,1)S(1)} %copy.39, bf16[768,2,128]{0,2,1:T(8,128)(2,1)S(1)} %bitcast.87, bf16[768,2,128]{2,0,1:T(8,128)(2,1)} %get-tuple-element.373, f32[768,2,128]{0,2,1:T(8,128)} %get-tuple-element.353, pred[]{:T(512)S(6)} %compare.3), kind=kOutput, calls=%fused_computation.14.clone.1 | convolution fusion | flops 612630528 | bytes 3342337 | tf_op jit(solution)/shard_map/while/body/eval_jaxpr/hqk,khe->qhe/dot_general | solution.py:74
  174.0 1.2 constant_dynamic-slice_fusion.3
  175.1 4.5 %fusion.55 = f32[768,2,128]{0,2,1:T(8,128)} fusion(bf16[768,2,128]{0,2,1:T(8,128)(2,1)S(1)} %bitcast.88, pred[768,768]{0,1:T(8,128)(4,1)S(1)} %copy.39, bf16[768,2,128]{0,2,1:T(8,128)(2,1)S(1)} %bitcast.87, bf16[768,2,128]{2,0,1:T(8,128)(2,1)} %get-tuple-element.373, f32[768,2,128]{0,2,1:T(8,128)} %get-tuple-element.353, pred[]{:T(512)S(6)} %compare.3), kind=kOutput, calls=%fused_computation.14.clone.1 | convolution fusion | flops 612630528 | bytes 3342337 | tf_op jit(solution)/shard_map/while/body/eval_jaxpr/hqk,khe->qhe/dot_general | solution.py:74
  183.0 1.2 constant_dynamic-slice_fusion.3
  184.2 4.5 %fusion.55 = f32[768,2,128]{0,2,1:T(8,128)} fusion(bf16[768,2,128]{0,2,1:T(8,128)(2,1)S(1)} %bitcast.88, pred[768,768]{0,1:T(8,128)(4,1)S(1)} %copy.39, bf16[768,2,128]{0,2,1:T(8,128)(2,1)S(1)} %bitcast.87, bf16[768,2,128]{2,0,1:T(8,128)(2,1)} %get-tuple-element.373, f32[768,2,128]{0,2,1:T(8,128)} %get-tuple-element.353, pred[]{:T(512)S(6)} %compare.3), kind=kOutput, calls=%fused_computation.14.clone.1 | convolution fusion | flops 612630528 | bytes 3342337 | tf_op jit(solution)/shard_map/while/body/eval_jaxpr/hqk,khe->qhe/dot_general | solution.py:74
  192.1 1.2 constant_dynamic-slice_fusion.3
  193.3 4.5 %fusion.55 = f32[768,2,128]{0,2,1:T(8,128)} fusion(bf16[768,2,128]{0,2,1:T(8,128)(2,1)S(1)} %bitcast.88, pred[768,768]{0,1:T(8,128)(4,1)S(1)} %copy.39, bf16[768,2,128]{0,2,1:T(8,128)(2,1)S(1)} %bitcast.87, bf16[768,2,128]{2,0,1:T(8,128)(2,1)} %get-tuple-element.373, f32[768,2,128]{0,2,1:T(8,128)} %get-tuple-element.353, pred[]{:T(512)S(6)} %compare.3), kind=kOutput, calls=%fused_computation.14.clone.1 | convolution fusion | flops 612630528 | bytes 3342337 | tf_op jit(solution)/shard_map/while/body/eval_jaxpr/hqk,khe->qhe/dot_general | solution.py:74
  201.2 1.2 constant_dynamic-slice_fusion.3
  202.4 4.5 %fusion.55 = f32[768,2,128]{0,2,1:T(8,128)} fusion(bf16[768,2,128]{0,2,1:T(8,128)(2,1)S(1)} %bitcast.88, pred[768,768]{0,1:T(8,128)(4,1)S(1)} %copy.39, bf16[768,2,128]{0,2,1:T(8,128)(2,1)S(1)} %bitcast.87, bf16[768,2,128]{2,0,1:T(8,128)(2,1)} %get-tuple-element.373, f32[768,2,128]{0,2,1:T(8,128)} %get-tuple-element.353, pred[]{:T(512)S(6)} %compare.3), kind=kOutput, calls=%fused_computation.14.clone.1 | convolution fusion | flops 612630528 | bytes 3342337 | tf_op jit(solution)/shard_map/while/body/eval_jaxpr/hqk,khe->qhe/dot_general | solution.py:74
  210.3 1.2 constant_dynamic-slice_fusion.3
  211.5 4.5 %fusion.55 = f32[768,2,128]{0,2,1:T(8,128)} fusion(bf16[768,2,128]{0,2,1:T(8,128)(2,1)S(1)} %bitcast.88, pred[768,768]{0,1:T(8,128)(4,1)S(1)} %copy.39, bf16[768,2,128]{0,2,1:T(8,128)(2,1)S(1)} %bitcast.87, bf16[768,2,128]{2,0,1:T(8,128)(2,1)} %get-tuple-element.373, f32[768,2,128]{0,2,1:T(8,128)} %get-tuple-element.353, pred[]{:T(512)S(6)} %compare.3), kind=kOutput, calls=%fused_computation.14.clone.1 | convolution fusion | flops 612630528 | bytes 3342337 | tf_op jit(solution)/shard_map/while/body/eval_jaxpr/hqk,khe->qhe/dot_general | solution.py:74
  219.4 1.2 constant_dynamic-slice_fusion.3
  220.5 4.5 %fusion.55 = f32[768,2,128]{0,2,1:T(8,128)} fusion(bf16[768,2,128]{0,2,1:T(8,128)(2,1)S(1)} %bitcast.88, pred[768,768]{0,1:T(8,128)(4,1)S(1)} %copy.39, bf16[768,2,128]{0,2,1:T(8,128)(2,1)S(1)} %bitcast.87, bf16[768,2,128]{2,0,1:T(8,128)(2,1)} %get-tuple-element.373, f32[768,2,128]{0,2,1:T(8,128)} %get-tuple-element.353, pred[]{:T(512)S(6)} %compare.3), kind=kOutput, calls=%fused_computation.14.clone.1 | convolution fusion | flops 612630528 | bytes 3342337 | tf_op jit(solution)/shard_map/while/body/eval_jaxpr/hqk,khe->qhe/dot_general | solution.py:74
  225.0 1.2 reduce_sum.38
  226.3 1.2 multiply_reduce_fusion
  227.5 1.4 fusion.36
  229.0 2.3 fusion.39
  231.3 43.6 %reduce-scatter.2.cloned.1.call-done = f32[768,256]{1,0:T(8,128)} async-done(((f32[768,1024]{1,0:T(8,128)}), f32[768,256]{1,0:T(8,128)}) %reduce-scatter.2.cloned.1.call-update) | async-done | bytes 786448 | tf_op jit(solution)/shard_map/reduce_scatter | solution.py:91
  274.9 2.1 add_convert_fusion
  (93 shorter events, 31.0 us)
Async XLA Ops:
  6.5 3.9 %copy-start = (bf16[4,1024,256]{2,1,0:T(8,128)(2,1)S(1)}, bf16[4,1024,256]{2,1,0:T(8,128)(2,1)}, u32[]{:S(2)}) copy-start(bf16[4,1024,256]{2,1,0:T(8,128)(2,1)} %param.13) | copy-start | bytes 6291460
  6.5 3.8 %copy-start.4 = (bf16[1024]{0:T(1024)(128)(2,1)S(1)}, bf16[1024]{0:T(1024)(128)(2,1)}, u32[]{:S(2)}) copy-start(bf16[1024]{0:T(1024)(128)(2,1)} %param.12) | copy-start | bytes 6148
  6.5 268.3 %reduce-scatter.2.cloned.1.call-start = ((), (), s32[]{:S(2)}) async-start(), calls=%async_computation.1 | async-start | bytes 3932160 | tf_op jit(solution)/shard_map/reduce_scatter | solution.py:91
  6.5 3.9 %copy-start.1 = (bf16[768,1024]{1,0:T(8,128)(2,1)S(1)}, bf16[768,1024]{1,0:T(8,128)(2,1)}, u32[]{:S(2)}) copy-start(bf16[768,1024]{1,0:T(8,128)(2,1)} %param.11) | copy-start | bytes 4718596
  16.8 21.4 %collective-permute-start = (bf16[2,768,256]{2,1,0:T(8,128)(2,1)}, bf16[2,768,256]{2,1,0:T(8,128)(2,1)S(1)}, u32[]{:S(2)}, u32[]{:S(2)}) collective-permute-start(bf16[2,768,256]{2,1,0:T(8,128)(2,1)} %get-tuple-element.331), channel_id=1, source_target_pairs={{0,4},{4,8},{8,12},{12,16},{16,20},{20,24},{24,28},{1,5},{5,9},{9,... | collective-permute-start | bytes 2359304 | tf_op jit(solution)/shard_map/while/body/eval_jaxpr/ppermute | solution.py:17
  42.4 20.5 %collective-permute-start = (bf16[2,768,256]{2,1,0:T(8,128)(2,1)}, bf16[2,768,256]{2,1,0:T(8,128)(2,1)S(1)}, u32[]{:S(2)}, u32[]{:S(2)}) collective-permute-start(bf16[2,768,256]{2,1,0:T(8,128)(2,1)} %get-tuple-element.331), channel_id=1, source_target_pairs={{0,4},{4,8},{8,12},{12,16},{16,20},{20,24},{24,28},{1,5},{5,9},{9,... | collective-permute-start | bytes 2359304 | tf_op jit(solution)/shard_map/while/body/eval_jaxpr/ppermute | solution.py:17
  67.0 19.6 %collective-permute-start = (bf16[2,768,256]{2,1,0:T(8,128)(2,1)}, bf16[2,768,256]{2,1,0:T(8,128)(2,1)S(1)}, u32[]{:S(2)}, u32[]{:S(2)}) collective-permute-start(bf16[2,768,256]{2,1,0:T(8,128)(2,1)} %get-tuple-element.331), channel_id=1, source_target_pairs={{0,4},{4,8},{8,12},{12,16},{16,20},{20,24},{24,28},{1,5},{5,9},{9,... | collective-permute-start | bytes 2359304 | tf_op jit(solution)/shard_map/while/body/eval_jaxpr/ppermute | solution.py:17
  90.6 18.6 %collective-permute-start = (bf16[2,768,256]{2,1,0:T(8,128)(2,1)}, bf16[2,768,256]{2,1,0:T(8,128)(2,1)S(1)}, u32[]{:S(2)}, u32[]{:S(2)}) collective-permute-start(bf16[2,768,256]{2,1,0:T(8,128)(2,1)} %get-tuple-element.331), channel_id=1, source_target_pairs={{0,4},{4,8},{8,12},{12,16},{16,20},{20,24},{24,28},{1,5},{5,9},{9,... | collective-permute-start | bytes 2359304 | tf_op jit(solution)/shard_map/while/body/eval_jaxpr/ppermute | solution.py:17
  113.4 17.7 %collective-permute-start = (bf16[2,768,256]{2,1,0:T(8,128)(2,1)}, bf16[2,768,256]{2,1,0:T(8,128)(2,1)S(1)}, u32[]{:S(2)}, u32[]{:S(2)}) collective-permute-start(bf16[2,768,256]{2,1,0:T(8,128)(2,1)} %get-tuple-element.331), channel_id=1, source_target_pairs={{0,4},{4,8},{8,12},{12,16},{16,20},{20,24},{24,28},{1,5},{5,9},{9,... | collective-permute-start | bytes 2359304 | tf_op jit(solution)/shard_map/while/body/eval_jaxpr/ppermute | solution.py:17
  135.3 16.8 %collective-permute-start = (bf16[2,768,256]{2,1,0:T(8,128)(2,1)}, bf16[2,768,256]{2,1,0:T(8,128)(2,1)S(1)}, u32[]{:S(2)}, u32[]{:S(2)}) collective-permute-start(bf16[2,768,256]{2,1,0:T(8,128)(2,1)} %get-tuple-element.331), channel_id=1, source_target_pairs={{0,4},{4,8},{8,12},{12,16},{16,20},{20,24},{24,28},{1,5},{5,9},{9,... | collective-permute-start | bytes 2359304 | tf_op jit(solution)/shard_map/while/body/eval_jaxpr/ppermute | solution.py:17
  156.2 5.4 %copy-start.3 = (s32[6,16]{1,0:T(8,128)S(1)}, s32[6,16]{1,0:T(8,128)}, u32[]{:S(2)}) copy-start(s32[6,16]{1,0:T(8,128)} %param.16) | copy-start | bytes 1156
  156.2 5.4 %copy-start.5 = (s32[6]{0:T(128)S(1)}, s32[6]{0:T(128)}, u32[]{:S(2)}) copy-start(s32[6]{0:T(128)} %param.17) | copy-start | bytes 76
  161.7 65.9 %copy-start.6 = (bf16[256]{0:T(256)(128)(2,1)S(1)}, bf16[256]{0:T(256)(128)(2,1)}, u32[]{:S(2)}) copy-start(bf16[256]{0:T(256)(128)(2,1)} %param.14) | copy-start | bytes 1540
  225.0 4.0 %copy-start.2 = (bf16[256,1024]{1,0:T(8,128)(2,1)S(1)}, bf16[256,1024]{1,0:T(8,128)(2,1)}, u32[]{:S(2)}) copy-start(bf16[256,1024]{1,0:T(8,128)(2,1)} %param.15) | copy-start | bytes 1572868
Sparse Core Ops, SparseCore 0:
  231.4 43.4 reduce-scatter.1
where the time goes:
time: 287 us; the launch traced here: 284 us
  waiting for transfers between devices  145 us (51%)
  local copies, waits for them, and re-layouts  49.2 us (17%)
  matrix products  35.7 us (12%)
  other arithmetic  22.4 us (8%)
  between operations  13.5 us (5%)
  starting transfers between devices  12.9 us (4%)
  loops' own time  4.82 us (2%)
    ppermute x6, waiting for transfers between devices, shifted(): return lax.ppermute(shard, axis, pairs)  102 us
    reduce_scatter x1, waiting for transfers between devices, body(): lax.psum_scatter(partial_terms, 'head', scatter_dimension=1, tiled=True)  43.6 us
    dot_general x7, matrix products, visit(): jnp.einsum('hqk,khe->qhe', weights, visit_values, preferred_element_type=...  30.9 us
    dynamic_update_slice x12, local copies, waits for them, and re-layouts, body(): last_one, earlier = lax.scan(advance, keys_values, None, length=reach_devs)  19.5 us
    ppermute x6, starting transfers between devices, shifted(): return lax.ppermute(shard, axis, pairs)  12.9 us
    slice x7, local copies, waits for them, and re-layouts, visit(): visit_keys = visiting[0].reshape(tok_rows, heads_dev, DH)  8.22 us
    and x7, local copies, waits for them, and re-layouts, visit(): allowed = member_rows & causal  7.14 us
  transfers between devices with their start and end apart: 7, of which 7 were waited for; matrix products, arithmetic and copies ran while one was open for 0% of the time, Pallas kernels for 0%

commit v1 on v0

v1 whole, which is shorter than its diff:
```python
import functools

import jax
import jax.numpy as jnp
from jax import lax
from jax.experimental import pallas as pl
from jax.experimental.pallas import tpu as pltpu
from jax.sharding import PartitionSpec as P

DH = 128
BLK = 128
WIN = 32
MAXK = 16
EPS = 1e-05
GROUP = 4

NT = (((1,), (1,)), ((), ()))


def silu(v):
    half = 0.5 * v
    return half * jnp.tanh(half) + half


def normed(rows, gain):
    floats = rows.astype(jnp.float32)
    centre = jnp.mean(floats, axis=-1, keepdims=True)
    off = floats - centre
    spread = jnp.mean(jnp.square(off), axis=-1, keepdims=True)
    return (off * lax.rsqrt(spread + EPS) * gain.astype(jnp.float32)).astype(jnp.bfloat16)


def norm_kernel(history_ref, gain_ref, out_ref):
    out_ref[...] = normed(history_ref[...], gain_ref[...])


def own_kernel(history_ref, gain_ref, w_ref, gate_ref, query_ref):
    here = normed(history_ref[...], gain_ref[...])
    gate_ref[...] = silu(jnp.dot(here, w_ref[0], preferred_element_type=jnp.float32)).astype(
        jnp.bfloat16
    )
    query_ref[...] = silu(jnp.dot(here, w_ref[2], preferred_element_type=jnp.float32)).astype(
        jnp.bfloat16
    )


def attend_kernel(
    slots_ref,
    live_ref,
    lists_ref,
    counts_ref,
    base_ref,
    normed_ref,
    w_ref,
    query_ref,
    gate_ref,
    gain_ref,
    out_ref,
    keys_ref,
    values_ref,
):
    step = pl.program_id(0)
    chunk = normed_ref.shape[0]
    sub = 2 * BLK
    cols = query_ref.shape[1]
    heads = cols // DH
    blocks_dev = counts_ref.shape[0]

    @pl.when(live_ref[step] > 0)
    def _():
        for part in range(chunk // sub):
            rows = normed_ref[pl.ds(part * sub, sub), :]
            at = pl.ds(step * chunk + part * sub, sub)
            keys_ref[at, :] = silu(
                jnp.dot(rows, w_ref[3], preferred_element_type=jnp.float32)
            ).astype(jnp.bfloat16)
            values_ref[at, :] = silu(
                jnp.dot(rows, w_ref[1], preferred_element_type=jnp.float32)
            ).astype(jnp.bfloat16)

    @pl.when(step == pl.num_programs(0) - 1)
    def _():
        base = base_ref[0]
        scale = 0.5 * DH ** (-0.5)
        causal = lax.broadcasted_iota(jnp.int32, (BLK, BLK), 1) <= lax.broadcasted_iota(
            jnp.int32, (BLK, BLK), 0
        )

        def one_block(i, unused):
            count = counts_ref[i]
            here = pl.ds(pl.multiple_of(i * BLK, BLK), BLK)
            query = query_ref[here, :]

            def group(j, sums):
                starts, scales = [], []
                for t in range(GROUP):
                    entry = j * GROUP + t
                    starts.append(pl.multiple_of((lists_ref[i, entry] - base) * BLK, BLK))
                    scales.append(jnp.where(entry < count, scale, 0.0))
                done = []
                for h in range(heads):
                    at = pl.ds(h * DH, DH)
                    keys = jnp.concatenate([keys_ref[pl.ds(s, BLK), at] for s in starts], axis=0)
                    values = jnp.concatenate(
                        [values_ref[pl.ds(s, BLK), at] for s in starts], axis=0
                    )
                    scores = lax.dot_general(
                        query[:, h * DH : (h + 1) * DH],
                        keys,
                        NT,
                        preferred_element_type=jnp.float32,
                    )
                    weights = []
                    for t in range(GROUP):
                        half = scores[:, t * BLK : (t + 1) * BLK] * scales[t]
                        weight = half * jnp.tanh(half) + half
                        if t == 0:
                            weight = jnp.where(causal | (j > 0), weight, 0.0)
                        weights.append(weight.astype(jnp.bfloat16))
                    done.append(
                        sums[h]
                        + jnp.dot(
                            jnp.concatenate(weights, axis=1),
                            values,
                            preferred_element_type=jnp.float32,
                        )
                    )
                return tuple(done)

            zero = tuple(jnp.zeros((BLK, DH), jnp.float32) for h in range(heads))
            sums = lax.fori_loop(0, (count + GROUP - 1) // GROUP, group, zero)
            for h in range(heads):
                at = pl.ds(h * DH, DH)
                centre = jnp.mean(sums[h], axis=-1, keepdims=True)
                off = sums[h] - centre
                spread = jnp.mean(jnp.square(off), axis=-1, keepdims=True)
                gated = (
                    off
                    * lax.rsqrt(spread + EPS)
                    * gain_ref[:, at].astype(jnp.float32)
                    * gate_ref[here, at].astype(jnp.float32)
                )
                out_ref[here, at] = gated.astype(jnp.bfloat16)
            return unused

        lax.fori_loop(0, blocks_dev, one_block, 0)


def out_kernel(gated_ref, w_ref, history_ref, out_ref):
    mixed = jnp.dot(gated_ref[...], w_ref[...], preferred_element_type=jnp.float32)
    out_ref[...] = (mixed + history_ref[...].astype(jnp.float32)).astype(jnp.bfloat16)


def shifted(shard, by):
    length = lax.axis_size("seq")
    return lax.ppermute(shard, "seq", [(i, i + by) for i in range(length - by)])


def body(history, ln_gain, w_in, out_gain, w_out, block_lists, counts):
    tok_rows, width = history.shape
    blocks_dev = counts.shape[0]
    cols = w_in.shape[2]
    n_seq, n_head = lax.axis_size("seq"), lax.axis_size("head")
    seq_index, head_index = lax.axis_index("seq"), lax.axis_index("head")
    reach = (WIN - 1 + blocks_dev - 1) // blocks_dev
    depth = reach + 1
    gain = ln_gain.reshape(1, width)

    share_rows = tok_rows // n_head
    share = pl.pallas_call(
        norm_kernel,
        grid=(1,),
        out_shape=jax.ShapeDtypeStruct((share_rows, width), jnp.bfloat16),
    )(lax.dynamic_slice_in_dim(history, head_index * share_rows, share_rows, 0), gain)
    steps = jnp.arange(depth, dtype=jnp.int32)
    sources = seq_index - reach + steps
    if n_seq <= depth + 1:
        window = lax.all_gather(share, ("seq", "head"), axis=0, tiled=True)
        slots = jnp.maximum(sources, 0)
    else:
        shares = jnp.stack([shifted(share, reach - d) for d in range(reach)] + [share])
        window = lax.all_gather(shares, "head", axis=1).reshape(depth * tok_rows, width)
        slots = steps
    live = (sources >= 0).astype(jnp.int32)

    gate, query = pl.pallas_call(
        own_kernel,
        grid=(3,),
        in_specs=[
            pl.BlockSpec((tok_rows // 3, width), lambda i: (i, 0)),
            pl.BlockSpec((1, width), lambda i: (0, 0)),
            pl.BlockSpec((4, width, cols), lambda i: (0, 0, 0)),
        ],
        out_specs=[pl.BlockSpec((tok_rows // 3, cols), lambda i: (i, 0))] * 2,
        out_shape=[jax.ShapeDtypeStruct((tok_rows, cols), jnp.bfloat16)] * 2,
        compiler_params=pltpu.CompilerParams(vmem_limit_bytes=48 << 20),
    )(history, gain, w_in)

    whole = lambda shape: pl.BlockSpec(shape, lambda i, *refs: (0,) * len(shape))
    gated = pl.pallas_call(
        attend_kernel,
        grid_spec=pltpu.PrefetchScalarGridSpec(
            num_scalar_prefetch=5,
            grid=(depth,),
            in_specs=[
                pl.BlockSpec((tok_rows, width), lambda i, slots, *refs: (slots[i], 0)),
                whole((4, width, cols)),
                whole((tok_rows, cols)),
                whole((tok_rows, cols)),
                whole((1, cols)),
            ],
            out_specs=whole((tok_rows, cols)),
            scratch_shapes=[pltpu.VMEM((depth * tok_rows, cols), jnp.bfloat16)] * 2,
        ),
        out_shape=jax.ShapeDtypeStruct((tok_rows, cols), jnp.bfloat16),
        compiler_params=pltpu.CompilerParams(vmem_limit_bytes=48 << 20),
    )(
        slots,
        live,
        block_lists,
        counts,
        ((seq_index - reach) * blocks_dev).reshape(1).astype(jnp.int32),
        window,
        w_in,
        query,
        gate,
        out_gain.reshape(1, cols),
    )

    w_mine = lax.all_to_all(w_out, "head", split_axis=1, concat_axis=0, tiled=True)
    all_gated = lax.all_gather(gated, "head", axis=1, tiled=True)
    out_cols = width // n_head
    residual = lax.dynamic_slice_in_dim(history, head_index * out_cols, out_cols, 1)
    return pl.pallas_call(
        out_kernel,
        grid=(3,),
        in_specs=[
            pl.BlockSpec((tok_rows // 3, all_gated.shape[1]), lambda i: (i, 0)),
            pl.BlockSpec(w_mine.shape, lambda i: (0, 0)),
            pl.BlockSpec((tok_rows // 3, out_cols), lambda i: (i, 0)),
        ],
        out_specs=pl.BlockSpec((tok_rows // 3, out_cols), lambda i: (i, 0)),
        out_shape=jax.ShapeDtypeStruct((tok_rows, out_cols), jnp.bfloat16),
        compiler_params=pltpu.CompilerParams(vmem_limit_bytes=48 << 20),
    )(all_gated, w_mine, residual)


def solution(mesh):
    placed = (
        P("seq", None),
        P(),
        P(None, None, "head"),
        P("head"),
        P("head", None),
        P("seq", None),
        P("seq"),
    )
    return jax.shard_map(
        body, mesh=mesh, in_specs=placed, out_specs=P("seq", "head"), check_vma=False
    )
```

time: 287 us -> 165 us (0.57)
  local copies, waits for them, and re-layouts: 49.2 us -> 9.35 us
  waiting for transfers between devices: 145 us -> 109 us
  matrix products: 35.7 us -> 0 us
  Pallas kernels: 0 us -> 26.8 us
  other arithmetic: 22.4 us -> 0.01 us
  starting transfers between devices: 12.9 us -> 3.72 us
  loops' own time: 4.82 us -> 0 us
    ppermute x6 -> x0, waiting for transfers between devices: 102 us -> none  [shifted(): return lax.ppermute(shard, axis, pairs)]
    all_gather x0 -> x2, waiting for transfers between devices: none -> 102 us  [the longest x1 90.4 us: body(): window = lax.all_gather(share, ('seq', 'head'), axis=0, tiled=True)]
    reduce_scatter x1 -> x0, waiting for transfers between devices: 43.6 us -> none  [body(): lax.psum_scatter(partial_terms, 'head', scatter_dimension=1, tiled=True)]
    dot_general x9 -> x0, matrix products: 35.7 us -> none  [the longest x7 30.9 us: visit(): jnp.einsum('hqk,khe->qhe', weights, visit_values, preferred_element_type=...]
    pallas_call x0 -> x4, Pallas kernels: none -> 26.8 us  [the longest x1 20.6 us: body(): pl.pallas_call(attend_kernel, grid_spec=pltpu.PrefetchScalarGridSpec(num_...]
    dynamic_update_slice x12 -> x0, local copies, waits for them, and re-layouts: 19.5 us -> none  [body(): last_one, earlier = lax.scan(advance, keys_values, None, length=reach_devs)]
    ppermute x6 -> x0, starting transfers between devices: 12.9 us -> none  [shifted(): return lax.ppermute(shard, axis, pairs)]
    slice x8 -> x0, local copies, waits for them, and re-layouts: 9.07 us -> none  [the longest x7 8.22 us: visit(): visit_keys = visiting[0].reshape(tok_rows, heads_dev, DH)]
  transfers between devices with their start and end apart: 7 -> 3, of which waited for: 7 -> 3; matrix products, arithmetic and copies ran while one was open for 0% -> 1% of each run, Pallas kernels for 0% -> 1%
where the time goes in v1:
time: 165 us; the launch traced here: 162 us
  waiting for transfers between devices  109 us (66%)
  Pallas kernels  26.8 us (16%)
  between operations  13.5 us (8%)
  local copies, waits for them, and re-layouts  9.35 us (6%)
  starting transfers between devices  3.72 us (2%)
    all_gather x1, waiting for transfers between devices, body(): window = lax.all_gather(share, ('seq', 'head'), axis=0, tiled=True)  90.4 us
    pallas_call x1, Pallas kernels, body(): pl.pallas_call(attend_kernel, grid_spec=pltpu.PrefetchScalarGridSpec(num_...  20.6 us
    all_gather x1, waiting for transfers between devices, body(): all_gated = lax.all_gather(gated, 'head', axis=1, tiled=True)  11.2 us
    all_to_all x1, waiting for transfers between devices, body(): lax.all_to_all(w_out, 'head', split_axis=1, concat_axis=0, tiled=True)  6.96 us
    unnamed x18, local copies, waits for them, and re-layouts  4.42 us
    all_to_all x1, starting transfers between devices, body(): lax.all_to_all(w_out, 'head', split_axis=1, concat_axis=0, tiled=True)  3.68 us
  transfers between devices with their start and end apart: 3, of which 3 were waited for; matrix products, arithmetic and copies ran while one was open for 1% of the time, Pallas kernels for 1%

profile of v1, /device:TPU:25, one launch (start us, length us, event | category | flops | bytes accessed | tf_op | source)
XLA Modules:
  0.0 162.0 jit_solution(1576677241233607593)
XLA Ops:
  6.5 0.0 all-gather.3.cloned.1.call-start
  6.5 1.3 reshape.13.gain_ref
  7.8 0.0 copy-start.4
  7.8 1.8 %constant_dynamic-slice_fusion.1.history_ref = bf16[192,1024]{1,0:T(8,128)(2,1)} fusion(bf16[768,1024]{1,0:T(8,128)(2,1)} %history_ref.1, s32[]{:T(128)S(6)} %select_n.6), kind=kLoop, calls=%fused_computation.3 | loop fusion | bytes 786436 | tf_op jit(solution)/shard_map/dynamic_slice | solution.py:174
  9.6 2.1 %shard_map.73 = bf16[192,1024]{1,0:T(8,128)(2,1)} custom-call(bf16[192,1024]{1,0:T(8,128)(2,1)} %constant_dynamic-slice_fusion.1.history_ref, bf16[1,1024]{1,0:T(2,128)(2,1)} %reshape.13.gain_ref), custom_call_target="tpu_custom_call" | custom-call | tf_op jit(solution)/shard_map/pallas_call | solution.py:170
  11.7 0.0 all-gather.3.cloned.1.call-update
  11.7 0.0 all-gather.5.cloned.1.call-start
  11.7 0.0 copy-done.4
  11.7 0.0 copy-start
  11.8 1.6 copy-done
  13.3 0.0 copy-start.2
  13.3 1.4 copy-done.2
  14.7 0.0 copy-start.8
  14.7 0.0 copy-start.1
  14.8 0.0 copy-start.5
  14.8 0.0 copy-start.6
  14.8 2.2 %shard_map.74 = (bf16[768,256]{1,0:T(8,128)(2,1)S(1)}, bf16[768,256]{1,0:T(8,128)(2,1)S(1)}) custom-call(bf16[768,1024]{1,0:T(8,128)(2,1)S(1)} %copy-done.2, bf16[1,1024]{1,0:T(2,128)(2,1)S(1)} %copy-done.4, bf16[4,1024,256]{2,1,0:T(8,128)(2,1)S(1)} %copy-done), custom_call_target="tpu_custom_call" | custom-call | tf_op jit(solution)/shard_map/pallas_call | solution.py:186
  17.0 0.0 copy-done.8
  17.0 90.4 %all-gather.3.cloned.1.call-done.normed_ref = bf16[6144,1024]{1,0:T(8,128)(2,1)} async-done(((bf16[192,1024]{1,0:T(8,128)(2,1)}), bf16[6144,1024]{1,0:T(8,128)(2,1)}) %all-gather.3.cloned.1.call-update) | async-done | bytes 12582928 | tf_op jit(solution)/shard_map/all_gather | solution.py:178
  107.4 0.0 copy-done.1
  107.5 0.0 copy-done.5
  107.5 0.0 copy-done.6
  107.5 0.0 copy-start.7
  107.5 20.6 %shard_map.75 = bf16[768,256]{1,0:T(8,128)(2,1)} custom-call(s32[7]{0:T(128)S(1)} %fusion.slots_ref, s32[7]{0:T(128)S(1)} %compare_convert_fusion.live_ref, s32[6,16]{1,0:T(8,128)S(1)} %copy-done.5, s32[6]{0:T(128)S(1)} %copy-done.6, s32[1]{0:T(128)} %bitcast.base_ref, bf16[6144,1024]{1,0:T(8,128)(2,1)} %all-gather.3.cloned.1.call-done.normed_ref, ...), custom_call_target="tpu_custom_call" | custom-call | tf_op jit(solution)/shard_map/pallas_call | solution.py:200
  128.1 0.0 all-gather.5.cloned.1.call-update
  128.1 0.0 copy-done.7
  128.1 0.9 copy.11
  129.0 3.7 %all-to-all-start = ((bf16[256,4,256]{2,0,1:T(8,128)(2,1)}), bf16[256,4,256]{2,0,1:T(8,128)(2,1)S(1)}, u32[]{:S(2)}, u32[]{:S(2)}) async-start(bf16[256,4,256]{2,0,1:T(8,128)(2,1)} %bitcast.7), calls=%async_computation | async-start | bytes 1048576 | tf_op jit(solution)/shard_map/all_to_all | solution.py:230
  132.6 1.0 constant_dynamic-slice_fusion.history_ref
  133.7 7.0 %all-to-all-done = bf16[256,4,256]{2,0,1:T(8,128)(2,1)S(1)} async-done(((bf16[256,4,256]{2,0,1:T(8,128)(2,1)}), bf16[256,4,256]{2,0,1:T(8,128)(2,1)S(1)}, u32[]{:S(2)}, u32[]{:S(2)}) %all-to-all-start) | async-done | bytes 524320 | tf_op jit(solution)/shard_map/all_to_all | solution.py:230
  140.6 11.2 %all-gather.5.cloned.1.call-done.gated_ref = bf16[768,1024]{1,0:T(8,128)(2,1)} async-done(((bf16[768,256]{1,0:T(8,128)(2,1)}), bf16[768,1024]{1,0:T(8,128)(2,1)}) %all-gather.5.cloned.1.call-update) | async-done | bytes 1572880 | tf_op jit(solution)/shard_map/all_gather | solution.py:231
  151.8 0.0 copy-start.3
  151.8 1.4 copy-done.3
  153.2 1.9 %shard_map.76 = bf16[768,256]{1,0:T(8,128)(2,1)} custom-call(bf16[768,1024]{1,0:T(8,128)(2,1)S(1)} %copy-done.3, bf16[1024,256]{1,0:T(8,128)(2,1)S(1)} %bitcast.8, bf16[768,256]{1,0:T(8,128)(2,1)S(1)} %constant_dynamic-slice_fusion.history_ref), custom_call_target="tpu_custom_call" | custom-call | tf_op jit(solution)/shard_map/pallas_call | solution.py:234
  (3 shorter events, 0.0 us)
Async XLA Ops:
  6.5 100.9 %all-gather.3.cloned.1.call-start = ((), (), s32[]{:S(2)}) async-start(), calls=%async_computation.1 | async-start | bytes 12976128 | tf_op jit(solution)/shard_map/all_gather | solution.py:178
  7.8 3.9 %copy-start.4 = (bf16[1,1024]{1,0:T(2,128)(2,1)S(1)}, bf16[1,1024]{1,0:T(2,128)(2,1)}, u32[]{:S(2)}) copy-start(bf16[1,1024]{1,0:T(2,128)(2,1)} %reshape.13.gain_ref) | copy-start | bytes 6148
  11.7 140.1 %all-gather.5.cloned.1.call-start = ((), (), s32[]{:S(2)}) async-start(), calls=%async_computation.2 | async-start | bytes 1966080 | tf_op jit(solution)/shard_map/all_gather | solution.py:231
  11.7 1.6 copy-start
  13.3 1.4 copy-start.2
  14.7 2.2 %copy-start.8 = (bf16[256]{0:T(256)(128)(2,1)S(1)}, bf16[256]{0:T(256)(128)(2,1)}, u32[]{:S(2)}) copy-start(bf16[256]{0:T(256)(128)(2,1)} %param.10) | copy-start | bytes 1540
  14.7 92.7 %copy-start.1 = (bf16[4,1024,256]{2,1,0:T(8,128)(2,1)S(1)}, bf16[4,1024,256]{2,1,0:T(8,128)(2,1)}, u32[]{:S(2)}) copy-start(bf16[4,1024,256]{2,1,0:T(8,128)(2,1)} %w_ref.3) | copy-start | bytes 6291460
  14.8 92.7 %copy-start.5 = (s32[6,16]{1,0:T(8,128)S(1)}, s32[6,16]{1,0:T(8,128)}, u32[]{:S(2)}) copy-start(s32[6,16]{1,0:T(8,128)} %lists_ref.1) | copy-start | bytes 1156
  14.8 92.7 %copy-start.6 = (s32[6]{0:T(128)S(1)}, s32[6]{0:T(128)}, u32[]{:S(2)}) copy-start(s32[6]{0:T(128)} %counts_ref.1) | copy-start | bytes 76
  107.5 20.6 %copy-start.7 = (bf16[256,1024]{1,0:T(8,128)(2,1)S(1)}, bf16[256,1024]{1,0:T(8,128)(2,1)}, u32[]{:S(2)}) copy-start(bf16[256,1024]{1,0:T(8,128)(2,1)} %param.11) | copy-start | bytes 1572868
  129.0 11.7 %all-to-all-start = ((bf16[256,4,256]{2,0,1:T(8,128)(2,1)}), bf16[256,4,256]{2,0,1:T(8,128)(2,1)S(1)}, u32[]{:S(2)}, u32[]{:S(2)}) async-start(bf16[256,4,256]{2,0,1:T(8,128)(2,1)} %bitcast.7), calls=%async_computation | async-start | bytes 1048576 | tf_op jit(solution)/shard_map/all_to_all | solution.py:230
  151.8 1.4 copy-start.3
Sparse Core Ops, SparseCore 0:
  11.8 95.6 all-gather.2
  128.2 23.5 all-gather.4

commit v2 on v0

v2 whole, which is shorter than its diff:
```python
import jax
import jax.numpy as jnp
from jax import lax
from jax.experimental import pallas as pl
from jax.experimental.pallas import tpu as pltpu
from jax.sharding import PartitionSpec as P

DH = 128
BLK = 128
WIN = 32
MAXK = 16
EPS = 1e-05
GROUP = 4

NT = (((1,), (1,)), ((), ()))
PARAMS = pltpu.CompilerParams(vmem_limit_bytes=48 << 20)


def silu(v):
    half = 0.5 * v
    return half * jnp.tanh(half) + half


def project(rows, w):
    return silu(jnp.dot(rows, w, preferred_element_type=jnp.float32)).astype(jnp.bfloat16)


def normed(rows, gain):
    floats = rows.astype(jnp.float32)
    centre = jnp.mean(floats, axis=-1, keepdims=True)
    off = floats - centre
    spread = jnp.mean(jnp.square(off), axis=-1, keepdims=True)
    return (off * lax.rsqrt(spread + EPS) * gain.astype(jnp.float32)).astype(jnp.bfloat16)


def norm_kernel(head_ref, history_ref, gain_ref, out_ref):
    out_ref[...] = normed(history_ref[...], gain_ref[...])


def own_kernel(history_ref, gain_ref, w_ref, gate_ref, values_ref, query_ref, keys_ref):
    here = normed(history_ref[...], gain_ref[...])
    query_ref[...] = project(here, w_ref[2])
    keys_ref[...] = project(here, w_ref[3])
    values_ref[...] = project(here, w_ref[1])
    gate_ref[...] = project(here, w_ref[0])


def list_pairs(base, lists_ref, counts_ref, first, blocks, pairs_ref, n):
    for b in range(blocks):

        def entry(t, n):
            g = lists_ref[b, t] - base
            pairs_ref[n] = (first + b) * 16 + g
            return n + jnp.where((g >= 0) & (g < blocks), 1, 0)

        n = lax.fori_loop(0, counts_ref[b], entry, n)
    return n


def attend(own, base, lists, counts, lists_x, counts_x, query_ref, keys_ref, values_ref, sums_ref, pairs_ref):
    blocks = counts.shape[0]
    heads = query_ref.shape[1] // DH
    scale = 0.5 * DH ** (-0.5)
    n = list_pairs(base, lists, counts, 0, blocks, pairs_ref, 0)
    n = list_pairs(base, lists_x, counts_x, blocks, blocks, pairs_ref, n)
    for t in range(GROUP):
        pairs_ref[n + t] = 0
    behind = lax.broadcasted_iota(jnp.int32, (BLK, BLK), 1) - lax.broadcasted_iota(
        jnp.int32, (BLK, BLK), 0
    )

    def group(j, unused):
        done = []
        for t in range(GROUP):
            code = pairs_ref[j * GROUP + t]
            b, g = code // 16, code % 16
            factor = jnp.where(j * GROUP + t < n, scale, 0.0)
            rows = pl.ds(pl.multiple_of(b * BLK, BLK), BLK)
            at = pl.ds(pl.multiple_of(g * BLK, BLK), BLK)
            for h in range(heads):
                cols = pl.ds(h * DH, DH)
                scores = lax.dot_general(
                    query_ref[rows, cols], keys_ref[at, cols], NT, preferred_element_type=jnp.float32
                )
                half = scores * factor
                weights = half * jnp.tanh(half) + half
                if own:
                    weights = jnp.where(behind <= jnp.where(b == g, 0, BLK), weights, 0.0)
                update = jnp.dot(
                    weights.astype(jnp.bfloat16),
                    values_ref[at, cols],
                    preferred_element_type=jnp.float32,
                )
                done.append((rows, cols, update))
        for rows, cols, update in done:
            sums_ref[rows, cols] += update
        return unused

    lax.fori_loop(0, (n + GROUP - 1) // GROUP, group, 0)


def own_attend_kernel(
    place, lists, counts, lists_x, counts_x, query_ref, query_x_ref, keys_ref, values_ref, sums_ref, both_ref, pairs_ref
):
    rows = query_ref.shape[0]
    both_ref[0:rows, :] = query_ref[...]
    both_ref[rows : 2 * rows, :] = query_x_ref[...]
    sums_ref[...] = jnp.zeros_like(sums_ref)
    attend(
        True, place[0] * counts.shape[0], lists, counts, lists_x, counts_x, both_ref, keys_ref, values_ref, sums_ref, pairs_ref
    )


def make_chunk_kernel(back, n_head, last):
    def kernel(place, lists, counts, lists_x, counts_x, *refs):
        pieces = refs[:n_head]
        w_keys_ref, w_values_ref, query_ref, query_x_ref, before_ref = refs[n_head : n_head + 5]
        if last:
            sums_ref, send_ref, total_ref, both_ref, keys_ref, values_ref, pairs_ref = refs[n_head + 5 :]
        else:
            total_ref, both_ref, keys_ref, values_ref, pairs_ref = refs[n_head + 5 :]
        rows, cols = query_ref.shape
        share = pieces[0].shape[0]
        source = place[0] - 2 * back
        total_ref[...] = before_ref[...]

        @pl.when(source >= 0)
        def _():
            both_ref[0:rows, :] = query_ref[...]
            both_ref[rows : 2 * rows, :] = query_x_ref[...]
            for m, piece in enumerate(pieces):
                at = pl.ds(pl.multiple_of((place[1] ^ m) * share, share), share)
                keys_ref[at, :] = project(piece[...], w_keys_ref[0])
                values_ref[at, :] = project(piece[...], w_values_ref[0])
            attend(
                False, source * counts.shape[0], lists, counts, lists_x, counts_x,
                both_ref, keys_ref, values_ref, total_ref, pairs_ref,
            )

        if last:
            sums_ref[...] = total_ref[0:rows, :]
            for h in range(cols // DH):
                at = pl.ds(h * DH, DH)
                part = total_ref[rows : 2 * rows, at]
                send_ref[:, at] = (part - jnp.mean(part, axis=-1, keepdims=True)).astype(jnp.bfloat16)

    return kernel


def finish_kernel(sums_ref, arrived_ref, gate_ref, gain_ref, out_ref):
    for h in range(sums_ref.shape[1] // DH):
        at = pl.ds(h * DH, DH)
        part = sums_ref[:, at]
        part = part - jnp.mean(part, axis=-1, keepdims=True) + arrived_ref[:, at].astype(jnp.float32)
        off = part - jnp.mean(part, axis=-1, keepdims=True)
        spread = jnp.mean(jnp.square(off), axis=-1, keepdims=True)
        out_ref[:, at] = (
            off
            * lax.rsqrt(spread + EPS)
            * gain_ref[:, at].astype(jnp.float32)
            * gate_ref[:, at].astype(jnp.float32)
        ).astype(jnp.bfloat16)


def out_kernel(place, *refs):
    *pieces, w_ref, history_ref, out_ref = refs
    cols = pieces[0].shape[1]
    mixed = history_ref[...].astype(jnp.float32)
    for m, piece in enumerate(pieces):
        at = pl.ds(pl.multiple_of((place[1] ^ m) * cols, cols), cols)
        mixed = mixed + jnp.dot(piece[...], w_ref[at, :], preferred_element_type=jnp.float32)
    out_ref[...] = mixed.astype(jnp.bfloat16)


def crossed(array, axis, bit):
    return lax.ppermute(array, axis, [(i, i ^ bit) for i in range(lax.axis_size(axis))])


def spread(piece):
    n = lax.axis_size("head")
    pieces = {0: piece}
    bit = n // 2
    while bit:
        pieces.update({m + bit: crossed(p, "head", bit) for m, p in list(pieces.items())})
        bit //= 2
    return [pieces[m] for m in range(n)]


def whole(shape):
    return pl.BlockSpec(shape, lambda *at: (0,) * len(shape))


def body(history, ln_gain, w_in, out_gain, w_out, block_lists, counts):
    tok_rows, width = history.shape
    blocks = counts.shape[0]
    cols = w_in.shape[2]
    n_seq, n_head = lax.axis_size("seq"), lax.axis_size("head")
    seq_index, head_index = lax.axis_index("seq"), lax.axis_index("head")
    planes = (WIN - 1 + 2 * blocks - 1) // (2 * blocks)
    gain = ln_gain.reshape(1, width)
    place = jnp.stack([seq_index, head_index]).astype(jnp.int32)
    rows_of = lambda n: jax.ShapeDtypeStruct((n, cols), jnp.bfloat16)
    n_pairs = 2 * blocks * MAXK + GROUP

    share_rows = tok_rows // n_head
    share = pl.pallas_call(
        norm_kernel,
        grid_spec=pltpu.PrefetchScalarGridSpec(
            num_scalar_prefetch=1,
            grid=(1,),
            in_specs=[pl.BlockSpec((share_rows, width), lambda i, place: (place[1], 0)), whole((1, width))],
            out_specs=whole((share_rows, width)),
        ),
        out_shape=jax.ShapeDtypeStruct((share_rows, width), jnp.bfloat16),
    )(place, history, gain)
    upward = [(i, i + 2) for i in range(n_seq - 2)]
    chunks = []
    for back in range(planes):
        share = lax.ppermute(share, "seq", upward)
        chunks.append(spread(share))
    w_mine = lax.all_to_all(w_out, "head", split_axis=1, concat_axis=0, tiled=True)

    part = tok_rows // 3
    gate, values, query, keys = pl.pallas_call(
        own_kernel,
        grid=(3,),
        in_specs=[
            pl.BlockSpec((part, width), lambda i: (i, 0)),
            pl.BlockSpec((1, width), lambda i: (0, 0)),
            whole((4, width, cols)),
        ],
        out_specs=[pl.BlockSpec((part, cols), lambda i: (i, 0))] * 4,
        out_shape=[rows_of(tok_rows)] * 4,
        compiler_params=PARAMS,
    )(history, gain, w_in)
    query_x = crossed(query, "seq", 1)
    told = crossed(jnp.concatenate([block_lists, counts[:, None]], axis=1), "seq", 1)
    scalars = (place, block_lists, counts, told[:, :MAXK], told[:, MAXK])

    sums_shape = jax.ShapeDtypeStruct((2 * tok_rows, cols), jnp.float32)
    sums = pl.pallas_call(
        own_attend_kernel,
        grid_spec=pltpu.PrefetchScalarGridSpec(
            num_scalar_prefetch=5,
            grid=(1,),
            in_specs=[whole((tok_rows, cols))] * 4,
            out_specs=whole(sums_shape.shape),
            scratch_shapes=[
                pltpu.VMEM((2 * tok_rows, cols), jnp.bfloat16),
                pltpu.SMEM((n_pairs,), jnp.int32),
            ],
        ),
        out_shape=sums_shape,
        compiler_params=PARAMS,
    )(*scalars, query, query_x, keys, values)

    for back, pieces in enumerate(chunks, start=1):
        last = back == planes
        if last:
            out_shape = [jax.ShapeDtypeStruct((tok_rows, cols), jnp.float32), rows_of(tok_rows)]
        else:
            out_shape = sums_shape
        sums = pl.pallas_call(
            make_chunk_kernel(back, n_head, last),
            grid_spec=pltpu.PrefetchScalarGridSpec(
                num_scalar_prefetch=5,
                grid=(1,),
                in_specs=[whole((share_rows, width))] * n_head
                + [
                    pl.BlockSpec((1, width, cols), lambda *at: (3, 0, 0)),
                    pl.BlockSpec((1, width, cols), lambda *at: (1, 0, 0)),
                    whole((tok_rows, cols)),
                    whole((tok_rows, cols)),
                    whole(sums_shape.shape),
                ],
                out_specs=[whole((tok_rows, cols))] * 2 if last else whole(sums_shape.shape),
                scratch_shapes=([pltpu.VMEM(sums_shape.shape, jnp.float32)] if last else [])
                + [
                    pltpu.VMEM((2 * tok_rows, cols), jnp.bfloat16),
                    pltpu.VMEM((tok_rows, cols), jnp.bfloat16),
                    pltpu.VMEM((tok_rows, cols), jnp.bfloat16),
                    pltpu.SMEM((n_pairs,), jnp.int32),
                ],
            ),
            out_shape=out_shape,
            compiler_params=PARAMS,
        )(*scalars, *pieces, w_in, w_in, query, query_x, sums)
    mine, send = sums
    arrived = crossed(send, "seq", 1)
    gated = pl.pallas_call(
        finish_kernel,
        grid=(1,),
        in_specs=[whole((tok_rows, cols))] * 3 + [whole((1, cols))],
        out_specs=whole((tok_rows, cols)),
        out_shape=rows_of(tok_rows),
        compiler_params=PARAMS,
    )(mine, arrived, gate, out_gain.reshape(1, cols))

    gated_pieces = spread(gated)
    out_cols = width // n_head
    return pl.pallas_call(
        out_kernel,
        grid_spec=pltpu.PrefetchScalarGridSpec(
            num_scalar_prefetch=1,
            grid=(3,),
            in_specs=[pl.BlockSpec((part, cols), lambda i, place: (i, 0))] * n_head
            + [
                whole(w_mine.shape),
                pl.BlockSpec((part, out_cols), lambda i, place: (i, place[1])),
            ],
            out_specs=pl.BlockSpec((part, out_cols), lambda i, place: (i, 0)),
        ),
        out_shape=jax.ShapeDtypeStruct((tok_rows, out_cols), jnp.bfloat16),
        compiler_params=PARAMS,
    )(place, *gated_pieces, w_mine, history)


def solution(mesh):
    placed = (
        P("seq", None),
        P(),
        P(None, None, "head"),
        P("head"),
        P("head", None),
        P("seq", None),
        P("seq"),
    )
    return jax.shard_map(
        body, mesh=mesh, in_specs=placed, out_specs=P("seq", "head"), check_vma=False
    )
```

time: 287 us -> 134 us (0.47)
  the two profiles are of different devices: /device:TPU:25 before, /device:TPU:8 now
where the time goes in v2:
time: 134 us; the launch traced here: 133 us
  waiting for transfers between devices  60.4 us (45%)
  Pallas kernels  45 us (34%)
  starting transfers between devices  22.2 us (17%)
  local copies, waits for them, and re-layouts  4.13 us (3%)
    ppermute x15, waiting for transfers between devices, crossed(): lax.ppermute(array, axis, [(i, i ^ bit) for i in range(lax.axis_size(axis...  38.2 us
    pallas_call x3, Pallas kernels, body(): pl.pallas_call(make_chunk_kernel(back, n_head, last), grid_spec=pltpu.Pre...  21.3 us
    ppermute x3, waiting for transfers between devices, body(): share = lax.ppermute(share, 'seq', upward)  17.9 us
    pallas_call x1, Pallas kernels, body(): pl.pallas_call(own_attend_kernel, grid_spec=pltpu.PrefetchScalarGridSpec(...  13.5 us
    ppermute x3, starting transfers between devices, body(): share = lax.ppermute(share, 'seq', upward)  10.4 us
    ppermute x15, starting transfers between devices, crossed(): lax.ppermute(array, axis, [(i, i ^ bit) for i in range(lax.axis_size(axis...  8.34 us
    all_to_all x1, waiting for transfers between devices, body(): lax.all_to_all(w_out, 'head', split_axis=1, concat_axis=0, tiled=True)  4.35 us
    pallas_call x1, Pallas kernels, body(): pl.pallas_call(out_kernel, grid_spec=pltpu.PrefetchScalarGridSpec(num_sca...  3.69 us
  transfers between devices with their start and end apart: 19, of which 9 were waited for; matrix products, arithmetic and copies ran while one was open for 1% of the time, Pallas kernels for 27%

profile of v2, /device:TPU:8, one launch (start us, length us, event | category | flops | bytes accessed | tf_op | source)
XLA Modules:
  0.0 132.6 jit_solution(17704003980139798133)
XLA Ops:
  0.0 1.4 %reshape.9.gain_ref = bf16[1,1024]{1,0:T(2,128)(2,1)} reshape(bf16[1024]{0:T(1024)(128)(2,1)} %param.8) | data formatting | bytes 4096 | tf_op jit(solution)/shard_map/reshape | solution.py:200
  1.4 0.7 pad_add_fusion.1.head_ref.place
  2.1 2.7 %shard_map.73 = bf16[192,1024]{1,0:T(8,128)(2,1)} custom-call(s32[2]{0:T(128)} %pad_add_fusion.1.head_ref.place, bf16[768,1024]{1,0:T(8,128)(2,1)} %refs_5_.7, bf16[1,1024]{1,0:T(2,128)(2,1)} %reshape.9.gain_ref), custom_call_target="tpu_custom_call" | custom-call | tf_op jit(solution)/shard_map/pallas_call | solution.py:206
  4.8 3.5 %collective-permute-start.1 = (bf16[192,1024]{1,0:T(8,128)(2,1)}, bf16[192,1024]{1,0:T(8,128)(2,1)S(1)}, u32[]{:S(2)}, u32[]{:S(2)}) collective-permute-start(bf16[192,1024]{1,0:T(8,128)(2,1)} %shard_map.73), channel_id=1, source_target_pairs={{0,8},{4,12},{8,16},{12,20},{16,24},{20,28},{1,9},{5,13},{9,17},{1... | collective-permute-start | bytes 1179656 | tf_op jit(solution)/shard_map/ppermute | solution.py:219
  8.3 9.5 %collective-permute-done.1.refs_0_ = bf16[192,1024]{1,0:T(8,128)(2,1)S(1)} collective-permute-done((bf16[192,1024]{1,0:T(8,128)(2,1)}, bf16[192,1024]{1,0:T(8,128)(2,1)S(1)}, u32[]{:S(2)}, u32[]{:S(2)}) %collective-permute-start.1) | collective-permute-done | bytes 393248 | tf_op jit(solution)/shard_map/ppermute | solution.py:219
  17.7 3.5 %collective-permute-start.2 = (bf16[192,1024]{1,0:T(8,128)(2,1)S(1)}, bf16[192,1024]{1,0:T(8,128)(2,1)S(1)}, u32[]{:S(2)}, u32[]{:S(2)}) collective-permute-start(bf16[192,1024]{1,0:T(8,128)(2,1)S(1)} %collective-permute-done.1.refs_0_), channel_id=1, source_target_pairs={{0,8},{4,12},{8,16},{12,20},{16,24},{20,28},{1,9},{5,13},{9,17},{1... | collective-permute-start | bytes 1179656 | tf_op jit(solution)/shard_map/ppermute | solution.py:219
  21.2 8.4 %collective-permute-done.2.refs_0_ = bf16[192,1024]{1,0:T(8,128)(2,1)S(1)} collective-permute-done((bf16[192,1024]{1,0:T(8,128)(2,1)S(1)}, bf16[192,1024]{1,0:T(8,128)(2,1)S(1)}, u32[]{:S(2)}, u32[]{:S(2)}) %collective-permute-start.2) | collective-permute-done | bytes 393248 | tf_op jit(solution)/shard_map/ppermute | solution.py:219
  29.6 3.5 %collective-permute-start.3 = (bf16[192,1024]{1,0:T(8,128)(2,1)S(1)}, bf16[192,1024]{1,0:T(8,128)(2,1)S(1)}, u32[]{:S(2)}, u32[]{:S(2)}) collective-permute-start(bf16[192,1024]{1,0:T(8,128)(2,1)S(1)} %collective-permute-done.2.refs_0_), channel_id=1, source_target_pairs={{0,8},{4,12},{8,16},{12,20},{16,24},{20,28},{1,9},{5,13},{9,17},{1... | collective-permute-start | bytes 1179656 | tf_op jit(solution)/shard_map/ppermute | solution.py:219
  33.1 0.1 copy.10
  33.2 0.1 pad_add_fusion
  33.2 1.5 %collective-permute-start = (s32[6,17]{1,0:T(8,128)S(1)}, s32[6,17]{1,0:T(8,128)S(1)}, u32[]{:S(2)}, u32[]{:S(2)}) collective-permute-start(s32[6,17]{1,0:T(8,128)S(1)} %pad_add_fusion), channel_id=1, source_target_pairs={{0,4},{4,0},{8,12},{12,8},{16,20},{20,16},{24,28},{28,24},{1,5},{5... | collective-permute-start | bytes 1232 | tf_op jit(solution)/shard_map/ppermute | solution.py:176
  34.7 1.6 %copy-done = bf16[4,1024,256]{2,1,0:T(8,128)(2,1)S(1)} copy-done((bf16[4,1024,256]{2,1,0:T(8,128)(2,1)S(1)}, bf16[4,1024,256]{2,1,0:T(8,128)(2,1)}, u32[]{:S(2)}) %copy-start) | copy-done | bytes 2097176
  36.3 3.1 %shard_map.74 = (bf16[768,256]{1,0:T(8,128)(2,1)S(1)}, bf16[768,256]{1,0:T(8,128)(2,1)S(1)}, bf16[768,256]{1,0:T(8,128)(2,1)S(1)}, bf16[768,256]{1,0:T(8,128)(2,1)S(1)}) custom-call(bf16[768,1024]{1,0:T(8,128)(2,1)S(1)} %copy-done.1, bf16[1,1024]{1,0:T(2,128)(2,1)S(1)} %copy-done.3, bf16[4,1024,256]{2,1,0:T(8,128)(2,1)S(1)} %copy-done), custom_call_target="tpu_custom_call" | custom-call | tf_op jit(solution)/shard_map/pallas_call | solution.py:224
  39.4 0.6 collective-permute-start.7
  40.0 1.5 %collective-permute-start.12 = (bf16[192,1024]{1,0:T(8,128)(2,1)S(1)}, bf16[192,1024]{1,0:T(8,128)(2,1)S(1)}, u32[]{:S(2)}, u32[]{:S(2)}) collective-permute-start(bf16[192,1024]{1,0:T(8,128)(2,1)S(1)} %collective-permute-done.1.refs_0_), channel_id=1, source_target_pairs={{0,2},{1,3},{2,0},{3,1},{4,6},{5,7},{6,4},{7,5},{8,10},{9,11},{10,... | collective-permute-start | bytes 1179656 | tf_op jit(solution)/shard_map/ppermute | solution.py:176
  41.6 0.5 collective-permute-start.9
  42.1 0.0 collective-permute-done
  42.1 0.0 collective-permute-start.11
  42.1 0.0 collective-permute-done.3.refs_0_
  42.1 1.6 %collective-permute-start.5 = (bf16[192,1024]{1,0:T(8,128)(2,1)S(1)}, bf16[192,1024]{1,0:T(8,128)(2,1)S(1)}, u32[]{:S(2)}, u32[]{:S(2)}) collective-permute-start(bf16[192,1024]{1,0:T(8,128)(2,1)S(1)} %collective-permute-done.3.refs_0_), channel_id=1, source_target_pairs={{0,2},{1,3},{2,0},{3,1},{4,6},{5,7},{6,4},{7,5},{8,10},{9,11},{10,... | collective-permute-start | bytes 1179656 | tf_op jit(solution)/shard_map/ppermute | solution.py:176
  43.7 4.3 %collective-permute-done.7.query_x_ref.refs_7_ = bf16[768,256]{1,0:T(8,128)(2,1)S(1)} collective-permute-done((bf16[768,256]{1,0:T(8,128)(2,1)S(1)}, bf16[768,256]{1,0:T(8,128)(2,1)S(1)}, u32[]{:S(2)}, u32[]{:S(2)}) %collective-permute-start.7) | collective-permute-done | bytes 393248 | tf_op jit(solution)/shard_map/ppermute | solution.py:176
  48.0 0.0 collective-permute-start.8
  48.0 4.1 %collective-permute-done.12.refs_2_ = bf16[192,1024]{1,0:T(8,128)(2,1)S(1)} collective-permute-done((bf16[192,1024]{1,0:T(8,128)(2,1)S(1)}, bf16[192,1024]{1,0:T(8,128)(2,1)S(1)}, u32[]{:S(2)}, u32[]{:S(2)}) %collective-permute-start.12) | collective-permute-done | bytes 393248 | tf_op jit(solution)/shard_map/ppermute | solution.py:176
  52.1 0.0 collective-permute-start.13
  52.1 8.4 %collective-permute-done.9.refs_2_ = bf16[192,1024]{1,0:T(8,128)(2,1)S(1)} collective-permute-done((bf16[192,1024]{1,0:T(8,128)(2,1)S(1)}, bf16[192,1024]{1,0:T(8,128)(2,1)S(1)}, u32[]{:S(2)}, u32[]{:S(2)}) %collective-permute-start.9) | collective-permute-done | bytes 393248 | tf_op jit(solution)/shard_map/ppermute | solution.py:176
  60.5 0.0 collective-permute-start.10
  60.5 0.0 collective-permute-done.11.refs_1_
  60.5 0.5 collective-permute-start.4
  61.0 4.1 %collective-permute-done.5.refs_2_ = bf16[192,1024]{1,0:T(8,128)(2,1)S(1)} collective-permute-done((bf16[192,1024]{1,0:T(8,128)(2,1)S(1)}, bf16[192,1024]{1,0:T(8,128)(2,1)S(1)}, u32[]{:S(2)}, u32[]{:S(2)}) %collective-permute-start.5) | collective-permute-done | bytes 393248 | tf_op jit(solution)/shard_map/ppermute | solution.py:176
  65.1 0.0 collective-permute-start.6
  65.1 0.2 slice_reduce_fusion.counts_x
  65.3 13.5 %shard_map.75.refs_8_ = f32[1536,256]{1,0:T(8,128)S(1)} custom-call(s32[2]{0:T(128)S(1)} %copy-done.4, s32[6,16]{1,0:T(8,128)S(1)} %copy-done.2, s32[6]{0:T(128)S(1)} %copy-done.5, s32[6,16]{1,0:T(8,128)S(1)} %bitcast.12, s32[6]{0:T(128)S(1)} %slice_reduce_fusion.counts_x, bf16[768,256]{1,0:T(8,128)(2,1)S(1)} %get-tuple-element.11.query_ref.refs_6_, ...), custom_call_target="tpu_custom_call" | custom-call | tf_op jit(solution)/shard_map/pallas_call | solution.py:241
  78.8 17.0 %shard_map.76.refs_8_ = f32[1536,256]{1,0:T(8,128)S(1)} custom-call(s32[2]{0:T(128)S(1)} %copy-done.4, s32[6,16]{1,0:T(8,128)S(1)} %copy-done.2, s32[6]{0:T(128)S(1)} %copy-done.5, s32[6,16]{1,0:T(8,128)S(1)} %bitcast.13, s32[6]{0:T(128)S(1)} %slice_reduce_fusion.counts_x, bf16[192,1024]{1,0:T(8,128)(2,1)S(1)} %collective-permute-done.1.refs_0_, ...), custom_call_target="tpu_custom_call" | custom-call | tf_op jit(solution)/shard_map/pallas_call | solution.py:263
  95.8 0.0 collective-permute-done.8.refs_1_
  95.8 2.0 %shard_map.77.refs_8_ = f32[1536,256]{1,0:T(8,128)S(1)} custom-call(s32[2]{0:T(128)S(1)} %copy-done.4, s32[6,16]{1,0:T(8,128)S(1)} %copy-done.2, s32[6]{0:T(128)S(1)} %copy-done.5, s32[6,16]{1,0:T(8,128)S(1)} %bitcast.14, s32[6]{0:T(128)S(1)} %slice_reduce_fusion.counts_x, bf16[192,1024]{1,0:T(8,128)(2,1)S(1)} %collective-permute-done.2.refs_0_, ...), custom_call_target="tpu_custom_call" | custom-call | tf_op jit(solution)/shard_map/pallas_call | solution.py:263
  97.8 0.0 copy-start.7
  97.9 2.3 %shard_map.78 = (f32[768,256]{1,0:T(8,128)S(1)}, bf16[768,256]{1,0:T(8,128)(2,1)S(1)}) custom-call(s32[2]{0:T(128)S(1)} %copy-done.4, s32[6,16]{1,0:T(8,128)S(1)} %copy-done.2, s32[6]{0:T(128)S(1)} %copy-done.5, s32[6,16]{1,0:T(8,128)S(1)} %bitcast.15, s32[6]{0:T(128)S(1)} %slice_reduce_fusion.counts_x, ...), custom_call_target="tpu_custom_call" | custom-call | tf_op jit(solution)/shard_map/pallas_call | solution.py:263
  100.2 0.0 copy-start.6
  100.2 0.1 collective-permute-start.14
  100.3 11.5 %collective-permute-done.14.arrived_ref = bf16[768,256]{1,0:T(8,128)(2,1)S(1)} collective-permute-done((bf16[768,256]{1,0:T(8,128)(2,1)S(1)}, bf16[768,256]{1,0:T(8,128)(2,1)S(1)}, u32[]{:S(2)}, u32[]{:S(2)}) %collective-permute-start.14) | collective-permute-done | bytes 393248 | tf_op jit(solution)/shard_map/ppermute | solution.py:176
  111.8 0.7 shard_map.79.refs_0_
  112.5 1.6 %collective-permute-start.16 = (bf16[768,256]{1,0:T(8,128)(2,1)S(1)}, bf16[768,256]{1,0:T(8,128)(2,1)S(1)}, u32[]{:S(2)}, u32[]{:S(2)}) collective-permute-start(bf16[768,256]{1,0:T(8,128)(2,1)S(1)} %shard_map.79.refs_0_), channel_id=1, source_target_pairs={{0,2},{1,3},{2,0},{3,1},{4,6},{5,7},{6,4},{7,5},{8,10},{9,11},{10,... | collective-permute-start | bytes 1179656 | tf_op jit(solution)/shard_map/ppermute | solution.py:176
  114.1 0.8 copy.14
  114.9 3.5 %all-to-all-start = ((bf16[256,4,256]{2,0,1:T(8,128)(2,1)}), bf16[256,4,256]{2,0,1:T(8,128)(2,1)S(1)}, u32[]{:S(2)}, u32[]{:S(2)}) async-start(bf16[256,4,256]{2,0,1:T(8,128)(2,1)} %bitcast.9), calls=%async_computation | async-start | bytes 1048576 | tf_op jit(solution)/shard_map/all_to_all | solution.py:221
  118.4 0.5 collective-permute-start.15
  118.9 5.7 %collective-permute-done.16.refs_2_ = bf16[768,256]{1,0:T(8,128)(2,1)S(1)} collective-permute-done((bf16[768,256]{1,0:T(8,128)(2,1)S(1)}, bf16[768,256]{1,0:T(8,128)(2,1)S(1)}, u32[]{:S(2)}, u32[]{:S(2)}) %collective-permute-start.16) | collective-permute-done | bytes 393248 | tf_op jit(solution)/shard_map/ppermute | solution.py:176
  124.6 4.4 %all-to-all-done = bf16[256,4,256]{2,0,1:T(8,128)(2,1)S(1)} async-done(((bf16[256,4,256]{2,0,1:T(8,128)(2,1)}), bf16[256,4,256]{2,0,1:T(8,128)(2,1)S(1)}, u32[]{:S(2)}, u32[]{:S(2)}) %all-to-all-start) | async-done | bytes 524320 | tf_op jit(solution)/shard_map/all_to_all | solution.py:221
  128.9 3.7 %shard_map.80 = bf16[768,256]{1,0:T(8,128)(2,1)} custom-call(s32[2]{0:T(128)S(1)} %copy-done.4, bf16[768,256]{1,0:T(8,128)(2,1)S(1)} %shard_map.79.refs_0_, bf16[768,256]{1,0:T(8,128)(2,1)S(1)} %collective-permute-done.15.refs_1_, bf16[768,256]{1,0:T(8,128)(2,1)S(1)} %collective-permute-done.16.refs_2_, bf16[768,256]{1,0:T(8,128)(2,1)} %collective-permute-done.17.refs_3_, ...), custom_call_target="tpu_custom_call" | custom-call | tf_op jit(solution)/shard_map/pallas_call | solution.py:301
  (21 shorter events, 0.0 us)
Async XLA Ops:
  0.0 34.7 %copy-start.1 = (bf16[768,1024]{1,0:T(8,128)(2,1)S(1)}, bf16[768,1024]{1,0:T(8,128)(2,1)}, u32[]{:S(2)}) copy-start(bf16[768,1024]{1,0:T(8,128)(2,1)} %refs_5_.7) | copy-start | bytes 4718596
  0.0 33.1 %copy-start.5 = (s32[6]{0:T(128)S(1)}, s32[6]{0:T(128)}, u32[]{:S(2)}) copy-start(s32[6]{0:T(128)} %counts.7) | copy-start | bytes 76
  0.0 33.2 %copy-start.2 = (s32[6,16]{1,0:T(8,128)S(1)}, s32[6,16]{1,0:T(8,128)}, u32[]{:S(2)}) copy-start(s32[6,16]{1,0:T(8,128)} %lists.7) | copy-start | bytes 1156
  1.4 33.3 %copy-start.3 = (bf16[1,1024]{1,0:T(2,128)(2,1)S(1)}, bf16[1,1024]{1,0:T(2,128)(2,1)}, u32[]{:S(2)}) copy-start(bf16[1,1024]{1,0:T(2,128)(2,1)} %reshape.9.gain_ref) | copy-start | bytes 6148
  4.8 12.9 %collective-permute-start.1 = (bf16[192,1024]{1,0:T(8,128)(2,1)}, bf16[192,1024]{1,0:T(8,128)(2,1)S(1)}, u32[]{:S(2)}, u32[]{:S(2)}) collective-permute-start(bf16[192,1024]{1,0:T(8,128)(2,1)} %shard_map.73), channel_id=1, source_target_pairs={{0,8},{4,12},{8,16},{12,20},{16,24},{20,28},{1,9},{5,13},{9,17},{1... | collective-permute-start | bytes 1179656 | tf_op jit(solution)/shard_map/ppermute | solution.py:219
  17.7 11.9 %collective-permute-start.2 = (bf16[192,1024]{1,0:T(8,128)(2,1)S(1)}, bf16[192,1024]{1,0:T(8,128)(2,1)S(1)}, u32[]{:S(2)}, u32[]{:S(2)}) collective-permute-start(bf16[192,1024]{1,0:T(8,128)(2,1)S(1)} %collective-permute-done.1.refs_0_), channel_id=1, source_target_pairs={{0,8},{4,12},{8,16},{12,20},{16,24},{20,28},{1,9},{5,13},{9,17},{1... | collective-permute-start | bytes 1179656 | tf_op jit(solution)/shard_map/ppermute | solution.py:219
  29.6 12.5 %collective-permute-start.3 = (bf16[192,1024]{1,0:T(8,128)(2,1)S(1)}, bf16[192,1024]{1,0:T(8,128)(2,1)S(1)}, u32[]{:S(2)}, u32[]{:S(2)}) collective-permute-start(bf16[192,1024]{1,0:T(8,128)(2,1)S(1)} %collective-permute-done.2.refs_0_), channel_id=1, source_target_pairs={{0,8},{4,12},{8,16},{12,20},{16,24},{20,28},{1,9},{5,13},{9,17},{1... | collective-permute-start | bytes 1179656 | tf_op jit(solution)/shard_map/ppermute | solution.py:219
  33.2 8.8 %collective-permute-start = (s32[6,17]{1,0:T(8,128)S(1)}, s32[6,17]{1,0:T(8,128)S(1)}, u32[]{:S(2)}, u32[]{:S(2)}) collective-permute-start(s32[6,17]{1,0:T(8,128)S(1)} %pad_add_fusion), channel_id=1, source_target_pairs={{0,4},{4,0},{8,12},{12,8},{16,20},{20,16},{24,28},{28,24},{1,5},{5... | collective-permute-start | bytes 1232 | tf_op jit(solution)/shard_map/ppermute | solution.py:176
  34.7 1.6 %copy-start = (bf16[4,1024,256]{2,1,0:T(8,128)(2,1)S(1)}, bf16[4,1024,256]{2,1,0:T(8,128)(2,1)}, u32[]{:S(2)}) copy-start(bf16[4,1024,256]{2,1,0:T(8,128)(2,1)} %refs_5_.6) | copy-start | bytes 6291460
  36.3 29.0 %copy-start.4 = (s32[2]{0:T(128)S(1)}, s32[2]{0:T(128)}, u32[]{:S(2)}) copy-start(s32[2]{0:T(128)} %pad_add_fusion.1.head_ref.place) | copy-start | bytes 28
  39.4 8.6 %collective-permute-start.7 = (bf16[768,256]{1,0:T(8,128)(2,1)S(1)}, bf16[768,256]{1,0:T(8,128)(2,1)S(1)}, u32[]{:S(2)}, u32[]{:S(2)}) collective-permute-start(bf16[768,256]{1,0:T(8,128)(2,1)S(1)} %get-tuple-element.11.query_ref.refs_6_), channel_id=1, source_target_pairs={{0,4},{4,0},{8,12},{12,8},{16,20},{20,16},{24,28},{28,24},{1,5},{5... | collective-permute-start | bytes 1179656 | tf_op jit(solution)/shard_map/ppermute | solution.py:176
  40.0 12.1 %collective-permute-start.12 = (bf16[192,1024]{1,0:T(8,128)(2,1)S(1)}, bf16[192,1024]{1,0:T(8,128)(2,1)S(1)}, u32[]{:S(2)}, u32[]{:S(2)}) collective-permute-start(bf16[192,1024]{1,0:T(8,128)(2,1)S(1)} %collective-permute-done.1.refs_0_), channel_id=1, source_target_pairs={{0,2},{1,3},{2,0},{3,1},{4,6},{5,7},{6,4},{7,5},{8,10},{9,11},{10,... | collective-permute-start | bytes 1179656 | tf_op jit(solution)/shard_map/ppermute | solution.py:176
  41.6 19.0 %collective-permute-start.9 = (bf16[192,1024]{1,0:T(8,128)(2,1)S(1)}, bf16[192,1024]{1,0:T(8,128)(2,1)S(1)}, u32[]{:S(2)}, u32[]{:S(2)}) collective-permute-start(bf16[192,1024]{1,0:T(8,128)(2,1)S(1)} %collective-permute-done.2.refs_0_), channel_id=1, source_target_pairs={{0,2},{1,3},{2,0},{3,1},{4,6},{5,7},{6,4},{7,5},{8,10},{9,11},{10,... | collective-permute-start | bytes 1179656 | tf_op jit(solution)/shard_map/ppermute | solution.py:176
  42.1 18.5 %collective-permute-start.11 = (bf16[192,1024]{1,0:T(8,128)(2,1)S(1)}, bf16[192,1024]{1,0:T(8,128)(2,1)S(1)}, u32[]{:S(2)}, u32[]{:S(2)}) collective-permute-start(bf16[192,1024]{1,0:T(8,128)(2,1)S(1)} %collective-permute-done.1.refs_0_), channel_id=1, source_target_pairs={{0,1},{1,0},{2,3},{3,2},{4,5},{5,4},{6,7},{7,6},{8,9},{9,8},{10,11... | collective-permute-start | bytes 1179656 | tf_op jit(solution)/shard_map/ppermute | solution.py:176
  42.1 23.0 %collective-permute-start.5 = (bf16[192,1024]{1,0:T(8,128)(2,1)S(1)}, bf16[192,1024]{1,0:T(8,128)(2,1)S(1)}, u32[]{:S(2)}, u32[]{:S(2)}) collective-permute-start(bf16[192,1024]{1,0:T(8,128)(2,1)S(1)} %collective-permute-done.3.refs_0_), channel_id=1, source_target_pairs={{0,2},{1,3},{2,0},{3,1},{4,6},{5,7},{6,4},{7,5},{8,10},{9,11},{10,... | collective-permute-start | bytes 1179656 | tf_op jit(solution)/shard_map/ppermute | solution.py:176
  48.0 47.8 %collective-permute-start.8 = (bf16[192,1024]{1,0:T(8,128)(2,1)S(1)}, bf16[192,1024]{1,0:T(8,128)(2,1)S(1)}, u32[]{:S(2)}, u32[]{:S(2)}) collective-permute-start(bf16[192,1024]{1,0:T(8,128)(2,1)S(1)} %collective-permute-done.2.refs_0_), channel_id=1, source_target_pairs={{0,1},{1,0},{2,3},{3,2},{4,5},{5,4},{6,7},{7,6},{8,9},{9,8},{10,11... | collective-permute-start | bytes 1179656 | tf_op jit(solution)/shard_map/ppermute | solution.py:176
  52.1 26.7 %collective-permute-start.13 = (bf16[192,1024]{1,0:T(8,128)(2,1)S(1)}, bf16[192,1024]{1,0:T(8,128)(2,1)S(1)}, u32[]{:S(2)}, u32[]{:S(2)}) collective-permute-start(bf16[192,1024]{1,0:T(8,128)(2,1)S(1)} %collective-permute-done.12.refs_2_), channel_id=1, source_target_pairs={{0,1},{1,0},{2,3},{3,2},{4,5},{5,4},{6,7},{7,6},{8,9},{9,8},{10,11... | collective-permute-start | bytes 1179656 | tf_op jit(solution)/shard_map/ppermute | solution.py:176
  60.5 35.3 %collective-permute-start.10 = (bf16[192,1024]{1,0:T(8,128)(2,1)S(1)}, bf16[192,1024]{1,0:T(8,128)(2,1)S(1)}, u32[]{:S(2)}, u32[]{:S(2)}) collective-permute-start(bf16[192,1024]{1,0:T(8,128)(2,1)S(1)} %collective-permute-done.9.refs_2_), channel_id=1, source_target_pairs={{0,1},{1,0},{2,3},{3,2},{4,5},{5,4},{6,7},{7,6},{8,9},{9,8},{10,11... | collective-permute-start | bytes 1179656 | tf_op jit(solution)/shard_map/ppermute | solution.py:176
  60.5 37.3 %collective-permute-start.4 = (bf16[192,1024]{1,0:T(8,128)(2,1)S(1)}, bf16[192,1024]{1,0:T(8,128)(2,1)S(1)}, u32[]{:S(2)}, u32[]{:S(2)}) collective-permute-start(bf16[192,1024]{1,0:T(8,128)(2,1)S(1)} %collective-permute-done.3.refs_0_), channel_id=1, source_target_pairs={{0,1},{1,0},{2,3},{3,2},{4,5},{5,4},{6,7},{7,6},{8,9},{9,8},{10,11... | collective-permute-start | bytes 1179656 | tf_op jit(solution)/shard_map/ppermute | solution.py:176
  65.1 32.7 %collective-permute-start.6 = (bf16[192,1024]{1,0:T(8,128)(2,1)S(1)}, bf16[192,1024]{1,0:T(8,128)(2,1)S(1)}, u32[]{:S(2)}, u32[]{:S(2)}) collective-permute-start(bf16[192,1024]{1,0:T(8,128)(2,1)S(1)} %collective-permute-done.5.refs_2_), channel_id=1, source_target_pairs={{0,1},{1,0},{2,3},{3,2},{4,5},{5,4},{6,7},{7,6},{8,9},{9,8},{10,11... | collective-permute-start | bytes 1179656 | tf_op jit(solution)/shard_map/ppermute | solution.py:176
  97.8 2.4 %copy-start.7 = (bf16[256]{0:T(256)(128)(2,1)S(1)}, bf16[256]{0:T(256)(128)(2,1)}, u32[]{:S(2)}) copy-start(bf16[256]{0:T(256)(128)(2,1)} %param.10) | copy-start | bytes 1540
  100.2 13.9 %copy-start.6 = (bf16[256,1024]{1,0:T(8,128)(2,1)S(1)}, bf16[256,1024]{1,0:T(8,128)(2,1)}, u32[]{:S(2)}) copy-start(bf16[256,1024]{1,0:T(8,128)(2,1)} %param.11) | copy-start | bytes 1572868
  100.2 11.6 %collective-permute-start.14 = (bf16[768,256]{1,0:T(8,128)(2,1)S(1)}, bf16[768,256]{1,0:T(8,128)(2,1)S(1)}, u32[]{:S(2)}, u32[]{:S(2)}) collective-permute-start(bf16[768,256]{1,0:T(8,128)(2,1)S(1)} %get-tuple-element.15), channel_id=1, source_target_pairs={{0,4},{4,0},{8,12},{12,8},{16,20},{20,16},{24,28},{28,24},{1,5},{5... | collective-permute-start | bytes 1179656 | tf_op jit(solution)/shard_map/ppermute | solution.py:176
  112.5 12.1 %collective-permute-start.16 = (bf16[768,256]{1,0:T(8,128)(2,1)S(1)}, bf16[768,256]{1,0:T(8,128)(2,1)S(1)}, u32[]{:S(2)}, u32[]{:S(2)}) collective-permute-start(bf16[768,256]{1,0:T(8,128)(2,1)S(1)} %shard_map.79.refs_0_), channel_id=1, source_target_pairs={{0,2},{1,3},{2,0},{3,1},{4,6},{5,7},{6,4},{7,5},{8,10},{9,11},{10,... | collective-permute-start | bytes 1179656 | tf_op jit(solution)/shard_map/ppermute | solution.py:176
  114.9 14.0 %all-to-all-start = ((bf16[256,4,256]{2,0,1:T(8,128)(2,1)}), bf16[256,4,256]{2,0,1:T(8,128)(2,1)S(1)}, u32[]{:S(2)}, u32[]{:S(2)}) async-start(bf16[256,4,256]{2,0,1:T(8,128)(2,1)} %bitcast.9), calls=%async_computation | async-start | bytes 1048576 | tf_op jit(solution)/shard_map/all_to_all | solution.py:221
  118.4 10.5 %collective-permute-start.15 = (bf16[768,256]{1,0:T(8,128)(2,1)S(1)}, bf16[768,256]{1,0:T(8,128)(2,1)S(1)}, u32[]{:S(2)}, u32[]{:S(2)}) collective-permute-start(bf16[768,256]{1,0:T(8,128)(2,1)S(1)} %shard_map.79.refs_0_), channel_id=1, source_target_pairs={{0,1},{1,0},{2,3},{3,2},{4,5},{5,4},{6,7},{7,6},{8,9},{9,8},{10,11... | collective-permute-start | bytes 1179656 | tf_op jit(solution)/shard_map/ppermute | solution.py:176
  124.6 4.4 %collective-permute-start.17 = (bf16[768,256]{1,0:T(8,128)(2,1)S(1)}, bf16[768,256]{1,0:T(8,128)(2,1)}, u32[]{:S(2)}, u32[]{:S(2)}) collective-permute-start(bf16[768,256]{1,0:T(8,128)(2,1)S(1)} %collective-permute-done.16.refs_2_), channel_id=1, source_target_pairs={{0,1},{1,0},{2,3},{3,2},{4,5},{5,4},{6,7},{7,6},{8,9},{9,8},{10,11... | collective-permute-start | bytes 1179656 | tf_op jit(solution)/shard_map/ppermute | solution.py:176
